TPU v7x, 256 devices: a whole 4x4x8 slice. The times are simulated.
256 devices in a mesh: seq: 16 (over x, y_hi, core), dp: 16 (over z, y_lo).
Axes of the slice: x: 4, y: 4 (y_hi: 2, y_lo: 2; y = y_hi * 2 + y_lo), z: 8, core: 2. Of those that a mesh axis runs over, the one named last changes fastest.
Arguments:
- frames: bfloat16 [16, 2048, 1024], P('dp', 'seq'), may hold values from -6 to 6
- lengths: int32 [16], P('dp'), may hold values from 1024 to 2048, as said below
- stretch_sizes: int32 [16], P('dp'), may hold values from 8 to 32, as said below
- look_ahead: int32 [16], P('dp'), may hold values from 1 to 8, as said below
- norm_one: float32 [1024], replicated, may hold values from 0.5 to 1.5
- norm_two: float32 [1024], replicated, may hold values from 0.5 to 1.5
- w_query: bfloat16 [1024, 1024], replicated, may hold values from -8 to 8
- w_key: bfloat16 [1024, 1024], replicated, may hold values from -1 to 1
- w_value: bfloat16 [1024, 1024], replicated, may hold values from -0.1875 to 0.1875
- w_out: bfloat16 [1024, 1024], replicated, may hold values from -0.1875 to 0.1875
- conv_kernel: bfloat16 [31, 1024], replicated, may hold values from -1 to 1
Outputs:
- full_output: bfloat16 [16, 2048, 1024], P('dp', 'seq')
- stretch_output: bfloat16 [16, 2048, 1024], P('dp', 'seq')
- kernel_grad: float32 [31, 1024], replicated
Inputs may be any that keep to these rules, and one draw needn't show every extreme that they name: `lengths`: utterance 0 has all 2048 frames. `stretch_sizes`: utterance 0 has stretch size 32. `look_ahead`: utterance 0 has preview 8.
All inputs are finite; a program needn't handle non-finite values.
Results may differ from a plain program's by a relative error of at most 0.0045.
The roundings to bfloat16 on the way count: a program that leaves them out, or rounds other values in their place, can miss the bound.
Values may be sent and summed in bfloat16 or wider, within the bound.
No kernel may reach another device: no remote copies, remote signals or barrier semaphores. Data moves between devices by JAX's collectives and lax.ppermute only.
A program may use at most 128 MiB of HBM per device.

v0:
```python
import math
import jax
import jax.numpy as jnp
from jax import lax
from jax.sharding import PartitionSpec as P

HEADS = 16
KERNEL = 31
LEFT = 64
HALO = 128
EPSILON = 1e-05
FLOOR_SCORE = -1e30


def with_halo(value, sides, width):
    for axis, dim in sides:
        size, length = (lax.axis_size(axis), value.shape[dim])
        up = [(i, (i + 1) % size) for i in range(size - 1)]
        down = [(j, i) for i, j in up]
        last = lax.slice_in_dim(value, length - width, length, axis=dim)
        leading = lax.slice_in_dim(value, 0, width, axis=dim)
        before = lax.ppermute(last, axis, up)
        after = lax.ppermute(leading, axis, down)
        value = jnp.concatenate([before, value, after], axis=dim)
    return value


def shifted(value, axis, by):
    length = lax.axis_size(axis)
    pairs = [(i, i + by) for i in range(length) if 0 <= i + by < length]
    return lax.ppermute(value, axis, pairs)


def layer_norm(values, gain_vector):
    values = values.astype(jnp.float32)
    center = values - jnp.mean(values, axis=-1, keepdims=True)
    spread = jnp.mean(center * center, axis=-1, keepdims=True)
    return center * lax.rsqrt(spread + EPSILON) * gain_vector


def fresh_state(row_count, head_count, depth_count):
    return (
        jnp.full((head_count, row_count), FLOOR_SCORE, jnp.float32),
        jnp.zeros((head_count, row_count), jnp.float32),
        jnp.zeros((row_count, head_count * depth_count), jnp.float32),
    )


def finish_state(state):
    highest, totals, summed = state
    row_count = summed.shape[0]
    head_count = totals.shape[0]
    mixed = summed.reshape(row_count, head_count, -1) / totals.T[:, :, None]
    return mixed.reshape(row_count, -1).astype(jnp.bfloat16)


def fold_keys(state, query3, query_pos, key3, value3, key_start, length, scale):
    highest, totals, summed = state
    key_count = key3.shape[0]
    scores = jnp.einsum("qhe,khe->hqk", query3, key3, preferred_element_type=jnp.float32) * scale
    key_pos = key_start + jnp.arange(key_count, dtype=jnp.int32)
    visible = (key_pos[None, :] < length) | (key_pos[None, :] == query_pos[:, None])
    scores = jnp.where(visible[None], scores, FLOOR_SCORE)
    new_high = jnp.maximum(highest, jnp.max(scores, axis=-1))
    factor = jnp.exp(highest - new_high)
    expo = jnp.where(visible[None], jnp.exp(scores - new_high[:, :, None]), 0.0)
    totals = totals * factor + jnp.sum(expo, axis=-1)
    adding = jnp.einsum(
        "hqk,khe->qhe", expo.astype(jnp.bfloat16), value3, preferred_element_type=jnp.float32
    )
    row_count, head_count, depth_count = adding.shape
    summed = summed.reshape(row_count, head_count, depth_count) * factor.T[:, :, None] + adding
    return (new_high, totals, summed.reshape(row_count, head_count * depth_count))


def fold_blocks(state, query3, query_pos, keys3, values3, length, scale):
    key_count = keys3.shape[0]
    block_width = math.gcd(key_count, 256)
    number = key_count // block_width
    key_blocks = keys3.reshape(number, block_width, keys3.shape[1], keys3.shape[2])
    value_blocks = values3.reshape(number, block_width, values3.shape[1], values3.shape[2])

    def advance(carry, inputs):
        index, key_block, value_block = inputs
        return (
            fold_keys(
                carry, query3, query_pos, key_block, value_block, index * block_width, length, scale
            ),
            None,
        )

    state, _ = lax.scan(
        advance, state, (jnp.arange(number, dtype=jnp.int32), key_blocks, value_blocks)
    )
    return state


def windowed(query3, key_ext3, value_ext3, first_pos, length, stretch, lookup, scale):
    query_count = query3.shape[0]
    block_rows = min(query_count, 512)
    number = query_count // block_rows
    span = block_rows + 2 * HALO

    def one_block(index):
        start = index * block_rows
        query_pos = first_pos + start + jnp.arange(block_rows, dtype=jnp.int32)
        key_pos = first_pos + start - HALO + jnp.arange(span, dtype=jnp.int32)
        begin = query_pos // stretch * stretch
        inside = (key_pos[None, :] >= begin[:, None] - LEFT) & (
            key_pos[None, :] < begin[:, None] + stretch + lookup
        )
        inside = inside & (key_pos[None, :] >= 0) & (key_pos[None, :] < length)
        visible = inside | (key_pos[None, :] == query_pos[:, None])
        scores = (
            jnp.einsum("qhe,khe->hqk", query3, key_ext3, preferred_element_type=jnp.float32) * scale
        )
        scores = jnp.where(visible[None], scores, FLOOR_SCORE)
        highest = jnp.max(scores, axis=-1, keepdims=True)
        expo = jnp.where(visible[None], jnp.exp(scores - highest), 0.0)
        totals = jnp.sum(expo, axis=-1)
        mixed = jnp.einsum(
            "hqk,khe->qhe",
            expo.astype(jnp.bfloat16),
            value_ext3,
            preferred_element_type=jnp.float32,
        )
        return (mixed / totals.T[:, :, None]).reshape(block_rows, -1).astype(jnp.bfloat16)

    return lax.map(one_block, jnp.arange(number, dtype=jnp.int32)).reshape(query_count, -1)


def per_device(
    frames,
    lengths,
    stretch_sizes,
    look_ahead,
    norm_one,
    norm_two,
    w_query,
    w_key,
    w_value,
    w_out,
    conv_kernel,
):
    source = frames[0]
    row_count, model_width = source.shape
    head_count = HEADS
    depth_count = model_width // head_count
    scale = float(depth_count) ** (-0.5)
    seq_place = lax.axis_index("seq")
    length = lengths[0]
    stretch = stretch_sizes[0]
    lookup = look_ahead[0]
    first_pos = seq_place * row_count
    query_pos = first_pos + jnp.arange(row_count, dtype=jnp.int32)
    normed = layer_norm(source, norm_one).astype(jnp.bfloat16)
    query = jnp.dot(normed, w_query, preferred_element_type=jnp.float32).astype(jnp.bfloat16)
    key_rows = jnp.dot(normed, w_key, preferred_element_type=jnp.float32).astype(jnp.bfloat16)
    value_rows = jnp.dot(normed, w_value, preferred_element_type=jnp.float32).astype(jnp.bfloat16)
    query3 = query.reshape(row_count, head_count, depth_count)
    key_piece = lax.all_gather(key_rows, "seq", axis=0, tiled=True)
    value_piece = lax.all_gather(value_rows, "seq", axis=0, tiled=True)
    piece_rows = key_piece.shape[0]
    state = fold_blocks(
        fresh_state(row_count, head_count, depth_count),
        query3,
        query_pos,
        key_piece.reshape(piece_rows, head_count, depth_count),
        value_piece.reshape(piece_rows, head_count, depth_count),
        length,
        scale,
    )
    context_full = finish_state(state)
    stacked = jnp.stack([key_rows, value_rows])
    extended = with_halo(stacked, (("seq", 1),), HALO)
    context_stretch = windowed(
        query3,
        extended[0].reshape(-1, head_count, depth_count),
        extended[1].reshape(-1, head_count, depth_count),
        first_pos,
        length,
        stretch,
        lookup,
        scale,
    )
    valid = (query_pos < length).astype(jnp.float32)
    kernel_taps = conv_kernel.astype(jnp.float32)
    projected = jnp.dot(
        jnp.concatenate([context_full, context_stretch], axis=0),
        w_out,
        preferred_element_type=jnp.float32,
    )
    residual_full = source.astype(jnp.float32) + projected[:row_count]
    residual_stretch = source.astype(jnp.float32) + projected[row_count:]
    input_full = (layer_norm(residual_full, norm_two) * valid[:, None]).astype(jnp.bfloat16)
    input_stretch = (layer_norm(residual_stretch, norm_two) * valid[:, None]).astype(jnp.bfloat16)
    padded_full = with_halo(input_full, (("seq", 0),), KERNEL // 2)
    carried = shifted(input_stretch[row_count - (KERNEL - 1) :], "seq", 1)
    padded_stretch = jnp.concatenate([carried, input_stretch], axis=0)
    conv_full = jnp.zeros((row_count, model_width), jnp.float32)
    conv_stretch = jnp.zeros((row_count, model_width), jnp.float32)
    for offset in range(KERNEL):
        conv_full = conv_full + kernel_taps[offset] * padded_full[
            offset : offset + row_count
        ].astype(jnp.float32)
        conv_stretch = conv_stretch + kernel_taps[offset] * padded_stretch[
            offset : offset + row_count
        ].astype(jnp.float32)
    output_full = residual_full + jax.nn.silu(conv_full)
    output_stretch = residual_stretch + jax.nn.silu(conv_stretch)
    push = (
        2.0 * (output_stretch - output_full) * valid[:, None] / jnp.sqrt(length.astype(jnp.float32))
    )
    sigma = jax.nn.sigmoid(conv_stretch)
    slope = push * sigma * (1.0 + conv_stretch * (1.0 - sigma))
    grad_local = jnp.stack(
        [
            jnp.sum(slope * padded_stretch[offset : offset + row_count].astype(jnp.float32), axis=0)
            for offset in range(KERNEL)
        ]
    )
    kernel_grad = lax.psum(grad_local, ("seq", "dp"))
    return (
        output_full.astype(jnp.bfloat16)[None],
        output_stretch.astype(jnp.bfloat16)[None],
        kernel_grad,
    )


def solution(mesh):
    in_specs = (P("dp", "seq", None), P("dp"), P("dp"), P("dp"), P(), P(), P(), P(), P(), P(), P())
    out_specs = (P("dp", "seq", None), P("dp", "seq", None), P())
    return jax.shard_map(
        per_device, mesh=mesh, in_specs=in_specs, out_specs=out_specs, check_vma=False
    )
```

profile of v0, /device:TPU:8, one launch (start us, length us, event | category | flops | bytes accessed | tf_op | source)
XLA Modules:
  0.0 529.4 jit_solution(953079403688141178)
XLA Ops:
  7.2 1.2 convert_reduce_fusion
  8.5 1.2 fusion.44
  9.7 2.9 convolution_convert_fusion.2
  12.7 2.8 convolution_convert_fusion
  15.6 1.9 pad_maximum_fusion.1
  17.4 2.6 collective-permute-start
  20.0 1.3 collective-permute-start.1
  23.2 2.1 convolution_convert_fusion.1
  27.8 1.4 pad_maximum_fusion
  29.2 1.0 fusion.184
  30.2 2.3 copy.28
  32.5 1.2 copy.27
  33.6 3.8 fusion.188
  37.4 2.9 fusion.36
  40.3 40.4 %all-gather.3.cloned.1.call-done = bf16[2048,1024]{1,0:T(8,128)(2,1)} async-done(((bf16[128,1024]{1,0:T(8,128)(2,1)}), bf16[2048,1024]{1,0:T(8,128)(2,1)}) %all-gather.3.cloned.1.call-update) | async-done | bytes 4194320 | tf_op jit(solution)/shard_map/all_gather | solution.py:161
  80.8 11.6 %reshape.276 = bf16[8,256,16,64]{3,2,1,0:T(8,128)(2,1)} reshape(bf16[2048,1024]{1,0:T(8,128)(2,1)} %all-gather.3.cloned.1.call-done) | data formatting | bytes 8388608 | tf_op jit(solution)/shard_map/reshape;reshape | solution.py:80
  92.3 10.4 %copy.25 = bf16[8,256,16,64]{1,3,2,0:T(8,128)(2,1)} copy(bf16[8,256,16,64]{3,2,1,0:T(8,128)(2,1)} %reshape.276) | data formatting | bytes 8388608
  102.7 41.3 %all-gather.5.cloned.1.call-done = bf16[2048,1024]{1,0:T(8,128)(2,1)} async-done(((bf16[128,1024]{1,0:T(8,128)(2,1)}), bf16[2048,1024]{1,0:T(8,128)(2,1)}) %all-gather.5.cloned.1.call-update) | async-done | bytes 4194320 | tf_op jit(solution)/shard_map/all_gather | solution.py:162
  144.0 11.6 %reshape.277 = bf16[8,256,16,64]{3,2,1,0:T(8,128)(2,1)} reshape(bf16[2048,1024]{1,0:T(8,128)(2,1)} %all-gather.5.cloned.1.call-done) | data formatting | bytes 8388608 | tf_op jit(solution)/shard_map/reshape;reshape | solution.py:81
  155.6 10.3 %copy.26 = bf16[8,256,16,64]{1,3,2,0:T(8,128)(2,1)} copy(bf16[8,256,16,64]{3,2,1,0:T(8,128)(2,1)} %reshape.277) | data formatting | bytes 8388608
  166.0 65.6 %while.5 = (s32[]{:T(128)}, f32[16,128]{1,0:T(8,128)S(1)}, f32[16,128]{1,0:T(8,128)S(1)}, f32[128,1024]{0,1:T(8,128)S(1)}, s32[8]{0:T(128)S(1)}, /*index=5*/s32[...) while((s32[]{:T(128)}, f32[16,128]{1,0:T(8,128)S(1)}, ...), condition=%wide.region_5.6_spmd.clone, body=%wide.region_2.5_spmd.clone.sunk | while | flops 141374336 | bytes 17306316 | solution.py:92
  168.0 2.9 fusion.211
  171.0 2.6 fusion.215
  176.2 2.9 fusion.211
  179.2 2.6 fusion.215
  184.4 2.9 fusion.211
  187.4 2.6 fusion.215
  192.6 2.9 fusion.211
  195.6 2.6 fusion.215
  200.8 2.9 fusion.211
  203.8 2.6 fusion.215
  209.0 2.9 fusion.211
  212.0 2.6 fusion.215
  217.2 2.9 fusion.211
  220.2 2.6 fusion.215
  225.4 2.9 fusion.211
  228.4 2.6 fusion.215
  231.6 1.7 fusion.108
  235.0 2.2 collective-permute-start.4
  237.8 3.8 collective-permute-start.2
  241.6 1.3 collective-permute-start.3
  243.5 1.5 collective-permute-done.3
  245.1 21.2 %fusion.106 = (f32[1024]{0:T(1024)S(1)}, f32[1024]{0:T(1024)S(1)}, f32[1024]{0:T(1024)S(1)}, f32[1024]{0:T(1024)S(1)}, f32[1024]{0:T(1024)S(1)}, /*index=5*/f32[...) fusion(bf16[128,1024]{1,0:T(8,128)(2,1)} %copy-done.3, ...), kind=kLoop, calls=%fused_computation.235 | loop fusion | flops 57138176 | bytes 3432964 | tf_op jit(solution)/shard_map/reduce_sum | solution.py:218
  266.9 1.3 fusion.83
  269.0 4.7 stack.139
  273.8 1.9 convert_bitcast_fusion.1
  275.7 245.6 %all-reduce.2.cloned.1.call-done = f32[31,1024]{1,0:T(8,128)} async-done(((f32[31,1024]{1,0:T(8,128)}), f32[31,1024]{1,0:T(8,128)}) %all-reduce.2.cloned.1.call-update) | async-done | bytes 126992 | tf_op jit(solution)/shard_map/psum | solution.py:222
  521.3 1.6 copy.50
  (150 shorter events, 22.5 us)
Async XLA Ops:
  7.2 224.5 %copy-start = (bf16[1024,1024]{1,0:T(8,128)(2,1)S(1)}, bf16[1024,1024]{1,0:T(8,128)(2,1)}, u32[]{:S(2)}) copy-start(bf16[1024,1024]{1,0:T(8,128)(2,1)} %param.22) | copy-start | bytes 6291460
  7.2 5.5 %copy-start.2 = (bf16[1,128,1024]{2,1,0:T(8,128)(2,1)S(1)}, bf16[1,128,1024]{2,1,0:T(8,128)(2,1)}, u32[]{:S(2)}) copy-start(bf16[1,128,1024]{2,1,0:T(8,128)(2,1)} %param.13) | copy-start | bytes 786436
  7.2 5.5 %copy-start.10 = (f32[1024]{0:T(1024)S(1)}, f32[1024]{0:T(1024)}, u32[]{:S(2)}) copy-start(f32[1024]{0:T(1024)} %param.17) | copy-start | bytes 12292
  7.2 73.6 %all-gather.3.cloned.1.call-start = ((), (), s32[]{:S(2)}) async-start(), calls=%async_computation | async-start | bytes 4456448 | tf_op jit(solution)/shard_map/all_gather | solution.py:161
  12.6 3.0 copy-start.5
  12.6 131.4 %all-gather.5.cloned.1.call-start = ((), (), s32[]{:S(2)}) async-start(), calls=%async_computation.1 | async-start | bytes 4456448 | tf_op jit(solution)/shard_map/all_gather | solution.py:162
  15.5 505.8 %all-reduce.2.cloned.1.call-start = ((), (), s32[]{:S(2)}) async-start(), calls=%async_computation.2 | async-start | bytes 262144 | tf_op jit(solution)/shard_map/psum | solution.py:222
  15.5 10.9 %copy-start.9 = (bf16[31,1024]{1,0:T(8,128)(2,1)S(1)}, bf16[31,1024]{1,0:T(8,128)(2,1)}, u32[]{:S(2)}) copy-start(bf16[31,1024]{1,0:T(8,128)(2,1)} %param.23) | copy-start | bytes 190468
  15.5 12.3 %copy-start.6 = (bf16[128,1024]{1,0:T(8,128)(2,1)S(1)}, bf16[128,1024]{1,0:T(8,128)(2,1)}, u32[]{:S(2)}) copy-start(bf16[128,1024]{1,0:T(8,128)(2,1)} %convolution_convert_fusion) | copy-start | bytes 786436
  17.4 10.4 %collective-permute-start = (bf16[2,128,1024]{2,1,0:T(8,128)(2,1)}, bf16[2,128,1024]{2,1,0:T(8,128)(2,1)}, u32[]{:S(2)}, u32[]{:S(2)}) collective-permute-start(bf16[2,128,1024]{2,1,0:T(8,128)(2,1)} %pad_maximum_fusion.1), channel_id=1, source_target_pairs={{0,16},{16,32},{32,48},{48,64},{64,80},{80,96},{96,112},{112,128},... | collective-permute-start | bytes 1572872 | tf_op jit(solution)/shard_map/ppermute | solution.py:22
  20.0 7.8 %collective-permute-start.1 = (bf16[2,128,1024]{2,1,0:T(8,128)(2,1)}, bf16[2,128,1024]{2,1,0:T(8,128)(2,1)}, u32[]{:S(2)}, u32[]{:S(2)}) collective-permute-start(bf16[2,128,1024]{2,1,0:T(8,128)(2,1)} %pad_maximum_fusion.1), channel_id=1, source_target_pairs={{16,0},{32,16},{48,32},{64,48},{80,64},{96,80},{112,96},{128,112},... | collective-permute-start | bytes 1572872 | tf_op jit(solution)/shard_map/ppermute | solution.py:23
  33.6 3.8 copy-start.8
  171.0 2.6 copy-start.1
  179.2 2.6 copy-start.1
  187.4 2.6 copy-start.1
  195.6 2.6 copy-start.1
  203.8 2.6 copy-start.1
  212.0 2.6 copy-start.1
  220.2 2.6 copy-start.1
  228.4 2.6 copy-start.1
  233.3 0.7 copy-start.11
  233.3 0.7 copy-start.12
  234.3 0.7 copy-start.3
  234.3 2.9 copy-start.7
  235.0 10.0 %collective-permute-start.4 = (bf16[30,1024]{1,0:T(8,128)(2,1)S(1)}, bf16[30,1024]{1,0:T(8,128)(2,1)S(1)}, u32[]{:S(2)}, u32[]{:S(2)}) collective-permute-start(bf16[30,1024]{1,0:T(8,128)(2,1)S(1)} %slice.576), channel_id=1, source_target_pairs={{0,16},{16,32},{32,48},{48,64},{64,80},{80,96},{96,112},{112,128},... | collective-permute-start | bytes 184328 | tf_op jit(solution)/shard_map/ppermute | solution.py:31
  237.8 5.7 %collective-permute-start.2 = (bf16[15,1024]{1,0:T(8,128)(2,1)}, bf16[15,1024]{1,0:T(8,128)(2,1)}, u32[]{:S(2)}, u32[]{:S(2)}) collective-permute-start(bf16[15,1024]{1,0:T(8,128)(2,1)} %get-tuple-element.207), channel_id=1, source_target_pairs={{0,16},{16,32},{32,48},{48,64},{64,80},{80,96},{96,112},{112,128},... | collective-permute-start | bytes 92168 | tf_op jit(solution)/shard_map/ppermute | solution.py:22
  241.6 3.4 collective-permute-start.3
  243.5 22.7 %copy-start.4 = (bf16[128,1024]{1,0:T(8,128)(2,1)S(1)}, bf16[128,1024]{1,0:T(8,128)(2,1)}, u32[]{:S(2)}) copy-start(bf16[128,1024]{1,0:T(8,128)(2,1)} %copy-done.3) | copy-start | bytes 786436
Sparse Core Ops, SparseCore 0:
  12.7 67.9 all-gather.2
  84.0 59.9 all-gather.4
  273.9 247.2 all-reduce.1
where the time goes:
time: 532 us; the launch traced here: 529 us
  waiting for transfers between devices  329 us (62%)
  local copies, waits for them, and re-layouts  62.4 us (12%)
  matrix products  60.6 us (11%)
  other arithmetic  44.4 us (8%)
  between operations  16.1 us (3%)
  starting transfers between devices  11.2 us (2%)
  loops' own time  5.82 us (1%)
    psum x1, waiting for transfers between devices, per_device(): kernel_grad = lax.psum(grad_local, ('seq', 'dp'))  246 us
    all_gather x1, waiting for transfers between devices, per_device(): value_piece = lax.all_gather(value_rows, 'seq', axis=0, tiled=True)  41.3 us
    all_gather x1, waiting for transfers between devices, per_device(): key_piece = lax.all_gather(key_rows, 'seq', axis=0, tiled=True)  40.4 us
    reduce_sum x4, other arithmetic, per_device(): jnp.sum(slope * padded_stretch[offset:offset + row_count].astype(jnp.floa...  24 us
    dot_general x8, matrix products, fold_keys(): jnp.einsum('qhe,khe->hqk', query3, key3, preferred_element_type=jnp.float32)  23.4 us
    unnamed x27, local copies, waits for them, and re-layouts  23.2 us
    dot_general x8, matrix products, fold_keys(): jnp.einsum('hqk,khe->qhe', expo.astype(jnp.bfloat16), value3, preferred_e...  21 us
    another operation x1, local copies, waits for them, and re-layouts, fold_blocks(): values3.reshape(number, block_width, values3.shape[1], values3.shape[2])  11.6 us
  transfers between devices with their start and end apart: 8, of which 4 were waited for; matrix products, arithmetic and copies ran while one was open for 9% of the time, Pallas kernels for 0%

commit v1 on v0

--- a/solution.py
+++ b/solution.py
@@ -219,7 +219,7 @@
             for offset in range(KERNEL)
         ]
     )
-    kernel_grad = lax.psum(grad_local, ("seq", "dp"))
+    kernel_grad = lax.psum(lax.psum(grad_local, "seq"), "dp")
     return (
         output_full.astype(jnp.bfloat16)[None],
         output_stretch.astype(jnp.bfloat16)[None],

time: 532 us -> 570 us (1.071)
  waiting for transfers between devices: 329 us -> 367 us
    psum x1 -> x2, waiting for transfers between devices: 246 us -> 283 us  [per_device(): kernel_grad = lax.psum(lax.psum(grad_local, 'seq'), 'dp')]
  transfers between devices with their start and end apart: 8 -> 9, of which waited for: 4 -> 5; matrix products, arithmetic and copies ran while one was open for 9% -> 8% of each run, Pallas kernels for 0% -> 0%
where the time goes in v1:
time: 570 us; the launch traced here: 567 us
  waiting for transfers between devices  367 us (64%)
  local copies, waits for them, and re-layouts  62.4 us (11%)
  matrix products  60.6 us (11%)
  other arithmetic  44.4 us (8%)
  between operations  16.1 us (3%)
  starting transfers between devices  11.2 us (2%)
  loops' own time  5.82 us (1%)
    psum x2, waiting for transfers between devices, per_device(): kernel_grad = lax.psum(lax.psum(grad_local, 'seq'), 'dp')  283 us
    all_gather x1, waiting for transfers between devices, per_device(): value_piece = lax.all_gather(value_rows, 'seq', axis=0, tiled=True)  41.3 us
    all_gather x1, waiting for transfers between devices, per_device(): key_piece = lax.all_gather(key_rows, 'seq', axis=0, tiled=True)  40.4 us
    reduce_sum x4, other arithmetic, per_device(): jnp.sum(slope * padded_stretch[offset:offset + row_count].astype(jnp.floa...  24 us
    dot_general x8, matrix products, fold_keys(): jnp.einsum('qhe,khe->hqk', query3, key3, preferred_element_type=jnp.float32)  23.4 us
    unnamed x27, local copies, waits for them, and re-layouts  23.2 us
    dot_general x8, matrix products, fold_keys(): jnp.einsum('hqk,khe->qhe', expo.astype(jnp.bfloat16), value3, preferred_e...  21 us
    another operation x1, local copies, waits for them, and re-layouts, fold_blocks(): values3.reshape(number, block_width, values3.shape[1], values3.shape[2])  11.6 us
  transfers between devices with their start and end apart: 9, of which 5 were waited for; matrix products, arithmetic and copies ran while one was open for 8% of the time, Pallas kernels for 0%

profile of v1, /device:TPU:8, one launch (start us, length us, event | category | flops | bytes accessed | tf_op | source)
XLA Modules:
  0.0 567.3 jit_solution(12646907175461427613)
XLA Ops:
  7.2 1.2 convert_reduce_fusion
  8.5 1.2 fusion.44
  9.7 2.9 convolution_convert_fusion.2
  12.7 2.8 convolution_convert_fusion
  15.6 1.9 pad_maximum_fusion.1
  17.4 2.6 collective-permute-start
  20.0 1.3 collective-permute-start.1
  23.2 2.1 convolution_convert_fusion.1
  27.8 1.4 pad_maximum_fusion
  30.2 2.3 copy.28
  32.5 1.2 copy.27
  33.6 3.8 fusion.188
  37.4 2.9 fusion.36
  40.3 40.4 %all-gather.3.cloned.1.call-done = bf16[2048,1024]{1,0:T(8,128)(2,1)} async-done(((bf16[128,1024]{1,0:T(8,128)(2,1)}), bf16[2048,1024]{1,0:T(8,128)(2,1)}) %all-gather.3.cloned.1.call-update) | async-done | bytes 4194320 | tf_op jit(solution)/shard_map/all_gather | solution.py:161
  80.8 11.6 %reshape.276 = bf16[8,256,16,64]{3,2,1,0:T(8,128)(2,1)} reshape(bf16[2048,1024]{1,0:T(8,128)(2,1)} %all-gather.3.cloned.1.call-done) | data formatting | bytes 8388608 | tf_op jit(solution)/shard_map/reshape;reshape | solution.py:80
  92.3 10.4 %copy.25 = bf16[8,256,16,64]{1,3,2,0:T(8,128)(2,1)} copy(bf16[8,256,16,64]{3,2,1,0:T(8,128)(2,1)} %reshape.276) | data formatting | bytes 8388608
  102.7 41.3 %all-gather.5.cloned.1.call-done = bf16[2048,1024]{1,0:T(8,128)(2,1)} async-done(((bf16[128,1024]{1,0:T(8,128)(2,1)}), bf16[2048,1024]{1,0:T(8,128)(2,1)}) %all-gather.5.cloned.1.call-update) | async-done | bytes 4194320 | tf_op jit(solution)/shard_map/all_gather | solution.py:162
  144.0 11.6 %reshape.277 = bf16[8,256,16,64]{3,2,1,0:T(8,128)(2,1)} reshape(bf16[2048,1024]{1,0:T(8,128)(2,1)} %all-gather.5.cloned.1.call-done) | data formatting | bytes 8388608 | tf_op jit(solution)/shard_map/reshape;reshape | solution.py:81
  155.6 10.3 %copy.26 = bf16[8,256,16,64]{1,3,2,0:T(8,128)(2,1)} copy(bf16[8,256,16,64]{3,2,1,0:T(8,128)(2,1)} %reshape.277) | data formatting | bytes 8388608
  166.0 65.6 %while.5 = (s32[]{:T(128)}, f32[16,128]{1,0:T(8,128)S(1)}, f32[16,128]{1,0:T(8,128)S(1)}, f32[128,1024]{0,1:T(8,128)S(1)}, s32[8]{0:T(128)S(1)}, /*index=5*/s32[...) while((s32[]{:T(128)}, f32[16,128]{1,0:T(8,128)S(1)}, ...), condition=%wide.region_5.6_spmd.clone, body=%wide.region_2.5_spmd.clone.sunk | while | flops 141374336 | bytes 17306316 | solution.py:92
  168.0 2.9 fusion.211
  171.0 2.6 fusion.215
  176.2 2.9 fusion.211
  179.2 2.6 fusion.215
  184.4 2.9 fusion.211
  187.4 2.6 fusion.215
  192.6 2.9 fusion.211
  195.6 2.6 fusion.215
  200.8 2.9 fusion.211
  203.8 2.6 fusion.215
  209.0 2.9 fusion.211
  212.0 2.6 fusion.215
  217.2 2.9 fusion.211
  220.2 2.6 fusion.215
  225.4 2.9 fusion.211
  228.4 2.6 fusion.215
  231.6 1.7 fusion.108
  235.0 2.2 collective-permute-start.4
  237.8 3.8 collective-permute-start.2
  241.6 1.3 collective-permute-start.3
  243.5 1.5 collective-permute-done.3
  245.1 21.2 %fusion.106 = (f32[1024]{0:T(1024)S(1)}, f32[1024]{0:T(1024)S(1)}, f32[1024]{0:T(1024)S(1)}, f32[1024]{0:T(1024)S(1)}, f32[1024]{0:T(1024)S(1)}, /*index=5*/f32[...) fusion(bf16[128,1024]{1,0:T(8,128)(2,1)} %copy-done.3, ...), kind=kLoop, calls=%fused_computation.235 | loop fusion | flops 57138176 | bytes 3432964 | tf_op jit(solution)/shard_map/reduce_sum | solution.py:218
  266.9 1.3 fusion.83
  269.0 4.7 stack.139
  273.9 146.6 %all-reduce.3.cloned.1.call-done = f32[31,1024]{1,0:T(8,128)} async-done(((f32[31,1024]{1,0:T(8,128)}), f32[31,1024]{1,0:T(8,128)}) %all-reduce.3.cloned.1.call-update) | async-done | bytes 126992 | tf_op jit(solution)/shard_map/psum | solution.py:222
  420.5 1.9 convert_bitcast_fusion.1
  422.4 136.8 %all-reduce.5.cloned.1.call-done = f32[31,1024]{1,0:T(8,128)} async-done(((f32[31,1024]{1,0:T(8,128)}), f32[31,1024]{1,0:T(8,128)}) %all-reduce.5.cloned.1.call-update) | async-done | bytes 126992 | tf_op jit(solution)/shard_map/psum | solution.py:222
  559.2 1.6 copy.51
  (153 shorter events, 23.5 us)
Async XLA Ops:
  7.2 224.5 %copy-start = (bf16[1024,1024]{1,0:T(8,128)(2,1)S(1)}, bf16[1024,1024]{1,0:T(8,128)(2,1)}, u32[]{:S(2)}) copy-start(bf16[1024,1024]{1,0:T(8,128)(2,1)} %param.22) | copy-start | bytes 6291460
  7.2 5.5 copy-start.2
  7.2 5.5 copy-start.10
  7.2 73.6 %all-gather.3.cloned.1.call-start = ((), (), s32[]{:S(2)}) async-start(), calls=%async_computation | async-start | bytes 4456448 | tf_op jit(solution)/shard_map/all_gather | solution.py:161
  12.6 3.0 copy-start.5
  12.6 131.4 %all-gather.5.cloned.1.call-start = ((), (), s32[]{:S(2)}) async-start(), calls=%async_computation.1 | async-start | bytes 4456448 | tf_op jit(solution)/shard_map/all_gather | solution.py:162
  15.5 405.0 %all-reduce.3.cloned.1.call-start = ((), (), s32[]{:S(2)}) async-start(), calls=%async_computation.2 | async-start | bytes 262144 | tf_op jit(solution)/shard_map/psum | solution.py:222
  15.5 10.9 %copy-start.9 = (bf16[31,1024]{1,0:T(8,128)(2,1)S(1)}, bf16[31,1024]{1,0:T(8,128)(2,1)}, u32[]{:S(2)}) copy-start(bf16[31,1024]{1,0:T(8,128)(2,1)} %param.23) | copy-start | bytes 190468
  15.5 12.3 %copy-start.6 = (bf16[128,1024]{1,0:T(8,128)(2,1)S(1)}, bf16[128,1024]{1,0:T(8,128)(2,1)}, u32[]{:S(2)}) copy-start(bf16[128,1024]{1,0:T(8,128)(2,1)} %convolution_convert_fusion) | copy-start | bytes 786436
  17.4 10.4 %collective-permute-start = (bf16[2,128,1024]{2,1,0:T(8,128)(2,1)}, bf16[2,128,1024]{2,1,0:T(8,128)(2,1)}, u32[]{:S(2)}, u32[]{:S(2)}) collective-permute-start(bf16[2,128,1024]{2,1,0:T(8,128)(2,1)} %pad_maximum_fusion.1), channel_id=1, source_target_pairs={{0,16},{16,32},{32,48},{48,64},{64,80},{80,96},{96,112},{112,128},... | collective-permute-start | bytes 1572872 | tf_op jit(solution)/shard_map/ppermute | solution.py:22
  20.0 7.8 %collective-permute-start.1 = (bf16[2,128,1024]{2,1,0:T(8,128)(2,1)}, bf16[2,128,1024]{2,1,0:T(8,128)(2,1)}, u32[]{:S(2)}, u32[]{:S(2)}) collective-permute-start(bf16[2,128,1024]{2,1,0:T(8,128)(2,1)} %pad_maximum_fusion.1), channel_id=1, source_target_pairs={{16,0},{32,16},{48,32},{64,48},{80,64},{96,80},{112,96},{128,112},... | collective-permute-start | bytes 1572872 | tf_op jit(solution)/shard_map/ppermute | solution.py:23
  33.6 3.8 copy-start.8
  171.0 2.6 copy-start.1
  179.2 2.6 copy-start.1
  187.4 2.6 copy-start.1
  195.6 2.6 copy-start.1
  203.8 2.6 copy-start.1
  212.0 2.6 copy-start.1
  220.2 2.6 copy-start.1
  228.4 2.6 copy-start.1
  233.3 0.7 copy-start.11
  233.3 0.7 copy-start.12
  234.3 0.7 copy-start.3
  234.3 2.9 copy-start.7
  235.0 10.0 %collective-permute-start.4 = (bf16[30,1024]{1,0:T(8,128)(2,1)S(1)}, bf16[30,1024]{1,0:T(8,128)(2,1)S(1)}, u32[]{:S(2)}, u32[]{:S(2)}) collective-permute-start(bf16[30,1024]{1,0:T(8,128)(2,1)S(1)} %slice.576), channel_id=1, source_target_pairs={{0,16},{16,32},{32,48},{48,64},{64,80},{80,96},{96,112},{112,128},... | collective-permute-start | bytes 184328 | tf_op jit(solution)/shard_map/ppermute | solution.py:31
  237.8 5.7 collective-permute-start.2
  241.6 3.4 collective-permute-start.3
  243.5 22.7 %copy-start.4 = (bf16[128,1024]{1,0:T(8,128)(2,1)S(1)}, bf16[128,1024]{1,0:T(8,128)(2,1)}, u32[]{:S(2)}) copy-start(bf16[128,1024]{1,0:T(8,128)(2,1)} %copy-done.3) | copy-start | bytes 786436
  273.8 285.4 %all-reduce.5.cloned.1.call-start = ((), (), s32[]{:S(2)}) async-start(), calls=%async_computation.3 | async-start | bytes 262144 | tf_op jit(solution)/shard_map/psum | solution.py:222
Sparse Core Ops, SparseCore 0:
  12.7 67.9 all-gather.2
  84.0 59.9 all-gather.4
  273.9 146.5 all-reduce.2
  423.1 136.0 all-reduce.4
